TPU v7x, 32 devices: a whole 2x2x4 slice. The times are simulated.
32 devices in a mesh: groups: 2 (over y), front: 4 (over z), batch: 2 (over x), line: 2 (over core).
Axes of the slice: x: 2, y: 2, z: 4, core: 2. Of those that a mesh axis runs over, the one named last changes fastest.
Arguments:
- injections: float32 [2048, 512], P('front', ('groups', 'batch')), parts along dimension 1, may hold values from -6 to 6
- switch_from: int32 [2, 512], P(None, ('groups', 'batch')), parts along dimension 1, may hold values from 0 to 2047
- switch_to: int32 [2, 512], P(None, ('groups', 'batch')), parts along dimension 1, may hold values from 0 to 2047
- switch_susc: float32 [2, 512], P(None, ('groups', 'batch')), parts along dimension 1, may hold values from 0.5 to 4
- coupling: float32 [2048, 512], P('front'), may hold values from -1 to 1
- pivot_inverse: float32 [2048, 512], P('front')
- branch_from: int32 [4096], P(('front', 'line')), may hold values from 0 to 2047, as said below
- branch_to: int32 [4096], P(('front', 'line')), may hold values from 0 to 2047, as said below
- branch_susc: float32 [4096], P(('front', 'line')), may hold values from 0.5 to 2
- branch_owner: int32 [4096, 1], P(('front', 'line')), may hold values from 0 to 7; in each aligned block of 512 rows (0 to 511, 512 to 1023, ...) at most 128 rows name the same one
- in_weight: float32 [128], replicated, may hold values from -4 to 4
- in_bias: float32 [128], replicated, may hold values from -1 to 1
- out_weight: bfloat16 [128, 128], replicated, may hold values from -0.5 to 0.5
Outputs:
- region_scores: bfloat16 [8, 512, 128], P(('front', 'line'), ('groups', 'batch')), parts along dimension 1
- angles: float32 [2048, 512], P('front', ('groups', 'batch')), parts along dimension 1
There are 2 independent parts, one for each index of `groups`. A program takes and returns all parts, laid end to end along the dimension named above; an argument that names none is the same for every part. Nothing has to cross between parts.
Inputs may be any that keep to these rules, and one draw needn't show every extreme that they name: `branch_from`: the bus of row r lies in slab s = r // 1024, between s * 512 and s * 512 + 511. `branch_to`: the bus of row r lies in slab s = r // 1024 or in slab s + 1. `branch_owner`: in each aligned block of 512 rows (the branches of one device) no owner is named by more than 128 rows.
All inputs are finite; a program needn't handle non-finite values.
Results may differ from a plain program's by a relative error of at most 0.005.
Values sent between devices are 32-bit elements; how exact they have to be, the bound alone decides.
A program may use at most 64 MiB of HBM per device.

v0:
```python
import jax
import jax.numpy as jnp
from jax import lax
from jax.sharding import PartitionSpec as P

K = 2
BR_DEV = 512


def from_behind(value, axis, by):
    count = lax.axis_size(axis)
    pairs = [(i, i + by) for i in range(count) if 0 <= i + by < count]
    return lax.ppermute(value, axis, pairs)


def product(operand, against):
    return jnp.dot(
        operand, against, precision=lax.Precision.HIGHEST, preferred_element_type=jnp.float32
    )


def centered_tanh(loadings, in_weight, in_bias):
    return jnp.tanh(loadings[..., None] * in_weight + in_bias) - jnp.tanh(in_bias)


def capacitance_solve(terms, switch_susc):
    switches = switch_susc.shape[0]
    factor = [[None] * switches for row_at in range(switches)]
    for row_at in range(switches):
        for col_at in range(row_at + 1):
            partial_sum = terms[row_at, 1 + col_at]
            if row_at == col_at:
                partial_sum = partial_sum + 1.0 / switch_susc[row_at]
            for inner_at in range(col_at):
                partial_sum = partial_sum - factor[row_at][inner_at] * factor[col_at][inner_at]
            if row_at == col_at:
                factor[row_at][col_at] = jnp.sqrt(partial_sum)
            else:
                factor[row_at][col_at] = partial_sum / factor[col_at][col_at]
    lower_part = []
    for row_at in range(switches):
        running = terms[row_at, 0]
        for inner_at in range(row_at):
            running = running - factor[row_at][inner_at] * lower_part[inner_at]
        lower_part.append(running / factor[row_at][row_at])
    weights = [None] * switches
    for row_at in reversed(range(switches)):
        running = lower_part[row_at]
        for inner_at in range(row_at + 1, switches):
            running = running - factor[inner_at][row_at] * weights[inner_at]
        weights[row_at] = running / factor[row_at][row_at]
    return jnp.stack(weights)


def body(
    injections,
    switch_from,
    switch_to,
    switch_susc,
    coupling,
    pivot_inverse,
    branch_from,
    branch_to,
    branch_susc,
    branch_owner,
    in_weight,
    in_bias,
    out_weight,
):
    fronts = lax.axis_size("front")
    front_at = lax.axis_index("front")
    slab_size = coupling.shape[1]
    topo_count = injections.shape[1]
    first_bus = front_at * slab_size
    bus_ids = first_bus + jnp.arange(slab_size, dtype=jnp.int32)
    from_hot = (bus_ids[:, None, None] == switch_from[None]).astype(jnp.float32)
    to_hot = (bus_ids[:, None, None] == switch_to[None]).astype(jnp.float32)
    incidence = from_hot - to_hot
    stacked = jnp.concatenate([injections[:, None, :], incidence], axis=1).reshape(slab_size, -1)

    def lower_step(step_at, current):
        arrived = from_behind(current, "front", 1)
        return stacked - product(coupling, arrived)

    lowered = lax.fori_loop(0, fronts - 1, lower_step, stacked)
    pivoted = product(pivot_inverse, lowered)

    def upper_step(step_at, current):
        arrived = from_behind(product(coupling.T, current), "front", -1)
        return pivoted - arrived

    solved = lax.fori_loop(0, fronts - 1, upper_step, pivoted)
    solved_cols = solved.reshape(slab_size, K + 1, topo_count)
    local_terms = jnp.einsum(
        "bit,bct->ict", incidence, solved_cols, precision=lax.Precision.HIGHEST
    )
    terms = lax.psum(local_terms, "front")
    weights = capacitance_solve(terms, switch_susc)
    angles = solved_cols[:, 0, :] - jnp.einsum(
        "bit,it->bt", solved_cols[:, 1:, :], weights, precision=lax.Precision.HIGHEST
    )
    following = from_behind(angles, "front", -1)
    joined = jnp.concatenate([angles, following], axis=0)
    flows = branch_susc[:, None] * (joined[branch_from - first_bus] - joined[branch_to - first_bus])
    owners = lax.axis_size(("front", "line"))
    capacity = 2 * BR_DEV // owners
    owner_ids = branch_owner[:, 0]
    owner_hot = (owner_ids[:, None] == jnp.arange(owners, dtype=jnp.int32)[None]).astype(jnp.int32)
    before = jnp.cumsum(owner_hot, axis=0) - owner_hot
    position = jnp.sum(before * owner_hot, axis=1)
    slot_ids = owner_ids * capacity + position
    dispatch = (jnp.arange(owners * capacity, dtype=jnp.int32)[:, None] == slot_ids[None]).astype(
        jnp.float32
    )
    outgoing = product(dispatch, flows).reshape(owners, capacity, topo_count)
    arrived = lax.all_to_all(outgoing, ("front", "line"), split_axis=0, concat_axis=0, tiled=True)
    slot_rows = arrived.reshape(-1, arrived.shape[2])
    span_size = 32
    blocks = slot_rows.reshape(-1, span_size, slot_rows.shape[1])

    def accumulate(running, slot_block):
        return (running + jnp.sum(centered_tanh(slot_block, in_weight, in_bias), axis=0), None)

    start_sum = jnp.zeros((slot_rows.shape[1], in_weight.shape[0]), jnp.float32)
    summed, unused = lax.scan(accumulate, start_sum, blocks)
    pooled = (summed * BR_DEV ** (-0.5)).astype(jnp.bfloat16)
    region_scores = jnp.dot(pooled, out_weight, preferred_element_type=jnp.float32).astype(
        jnp.bfloat16
    )
    return (region_scores[None], angles)


def solution(mesh):
    in_specs = (
        P("front", ("groups", "batch")),
        P(None, ("groups", "batch")),
        P(None, ("groups", "batch")),
        P(None, ("groups", "batch")),
        P("front", None),
        P("front", None),
        P(("front", "line")),
        P(("front", "line")),
        P(("front", "line")),
        P(("front", "line"), None),
        P(),
        P(),
        P(),
    )
    out_specs = (P(("front", "line"), ("groups", "batch"), None), P("front", ("groups", "batch")))
    return jax.shard_map(body, mesh=mesh, in_specs=in_specs, out_specs=out_specs, check_vma=False)
```

profile of v0, /device:TPU:0, one launch (start us, length us, event | category | flops | bytes accessed | tf_op | source)
XLA Modules:
  0.0 243.3 jit_solution(18174583019754320143)
XLA Ops:
  4.5 73.9 %while.32 = (s32[]{:T(128)}, f32[512,384]{1,0:T(8,128)}, f32[512,512]{1,0:T(8,128)S(1)}, f32[512,384]{1,0:T(8,128)S(1)}, s32[]{:T(128)}) while((s32[]{:T(128)}, f32[512,384]{1,0:T(8,128)}, f32[512,512]{1,0:T(8,128)S(1)}, f32[512,384]{1,0:T(8,128)S(1)}, s32[]{:T(128)}) %tuple.77), condition=%wide.region_4.0_spmd, body=%wide.region_3.0_spmd.sunk | while | flops 1208156160 | bytes 6553701 | solution.py:85
  4.5 5.8 %collective-permute-start = (f32[512,384]{1,0:T(8,128)}, f32[512,384]{1,0:T(8,128)}, u32[]{:S(2)}, u32[]{:S(2)}) collective-permute-start(f32[512,384]{1,0:T(8,128)} %get-tuple-element.274), channel_id=1, source_target_pairs={{0,4},{4,8},{8,12},{1,5},{5,9},{9,13},{2,6},{6,10},{10,14},{3,7},{... | collective-permute-start | bytes 2359304 | tf_op jit(solution)/shard_map/while/body/eval_jaxpr/ppermute | solution.py:13
  10.3 16.2 %collective-permute-done = f32[512,384]{1,0:T(8,128)} collective-permute-done((f32[512,384]{1,0:T(8,128)}, f32[512,384]{1,0:T(8,128)}, u32[]{:S(2)}, u32[]{:S(2)}) %collective-permute-start) | collective-permute-done | bytes 786464 | tf_op jit(solution)/shard_map/while/body/eval_jaxpr/ppermute | solution.py:13
  26.6 3.8 %convolution_subtract_fusion.2 = f32[512,384]{1,0:T(8,128)} fusion(f32[512,384]{1,0:T(8,128)S(1)} %get-tuple-element.281, f32[512,512]{1,0:T(8,128)S(1)} %get-tuple-element.280, f32[512,384]{1,0:T(8,128)} %collective-permute-done), kind=kOutput, calls=%fused_computation.2.clone.1 | convolution fusion | flops 1208156160 | bytes 3407872 | tf_op jit(solution)/shard_map/while/body/eval_jaxpr/dot_general | solution.py:17
  30.4 5.3 %collective-permute-start = (f32[512,384]{1,0:T(8,128)}, f32[512,384]{1,0:T(8,128)}, u32[]{:S(2)}, u32[]{:S(2)}) collective-permute-start(f32[512,384]{1,0:T(8,128)} %get-tuple-element.274), channel_id=1, source_target_pairs={{0,4},{4,8},{8,12},{1,5},{5,9},{9,13},{2,6},{6,10},{10,14},{3,7},{... | collective-permute-start | bytes 2359304 | tf_op jit(solution)/shard_map/while/body/eval_jaxpr/ppermute | solution.py:13
  35.7 15.4 %collective-permute-done = f32[512,384]{1,0:T(8,128)} collective-permute-done((f32[512,384]{1,0:T(8,128)}, f32[512,384]{1,0:T(8,128)}, u32[]{:S(2)}, u32[]{:S(2)}) %collective-permute-start) | collective-permute-done | bytes 786464 | tf_op jit(solution)/shard_map/while/body/eval_jaxpr/ppermute | solution.py:13
  51.0 3.8 %convolution_subtract_fusion.2 = f32[512,384]{1,0:T(8,128)} fusion(f32[512,384]{1,0:T(8,128)S(1)} %get-tuple-element.281, f32[512,512]{1,0:T(8,128)S(1)} %get-tuple-element.280, f32[512,384]{1,0:T(8,128)} %collective-permute-done), kind=kOutput, calls=%fused_computation.2.clone.1 | convolution fusion | flops 1208156160 | bytes 3407872 | tf_op jit(solution)/shard_map/while/body/eval_jaxpr/dot_general | solution.py:17
  54.9 5.3 %collective-permute-start = (f32[512,384]{1,0:T(8,128)}, f32[512,384]{1,0:T(8,128)}, u32[]{:S(2)}, u32[]{:S(2)}) collective-permute-start(f32[512,384]{1,0:T(8,128)} %get-tuple-element.274), channel_id=1, source_target_pairs={{0,4},{4,8},{8,12},{1,5},{5,9},{9,13},{2,6},{6,10},{10,14},{3,7},{... | collective-permute-start | bytes 2359304 | tf_op jit(solution)/shard_map/while/body/eval_jaxpr/ppermute | solution.py:13
  60.1 14.4 %collective-permute-done = f32[512,384]{1,0:T(8,128)} collective-permute-done((f32[512,384]{1,0:T(8,128)}, f32[512,384]{1,0:T(8,128)}, u32[]{:S(2)}, u32[]{:S(2)}) %collective-permute-start) | collective-permute-done | bytes 786464 | tf_op jit(solution)/shard_map/while/body/eval_jaxpr/ppermute | solution.py:13
  74.5 3.8 %convolution_subtract_fusion.2 = f32[512,384]{1,0:T(8,128)} fusion(f32[512,384]{1,0:T(8,128)S(1)} %get-tuple-element.281, f32[512,512]{1,0:T(8,128)S(1)} %get-tuple-element.280, f32[512,384]{1,0:T(8,128)} %collective-permute-done), kind=kOutput, calls=%fused_computation.2.clone.1 | convolution fusion | flops 1208156160 | bytes 3407872 | tf_op jit(solution)/shard_map/while/body/eval_jaxpr/dot_general | solution.py:17
  78.4 4.7 %convolution_bitcast_fusion = f32[512,384]{0,1:T(8,128)} fusion(f32[512,384]{1,0:T(8,128)} %get-tuple-element.98, f32[512,512]{1,0:T(8,128)S(1)} %copy-done), kind=kOutput, calls=%fused_computation.8 | convolution fusion | flops 1207959552 | bytes 2621440 | tf_op jit(solution)/shard_map/dot_general | solution.py:17
  83.1 1.4 copy.34
  85.4 72.7 %while.33 = (s32[]{:T(128)}, f32[512,384]{1,0:T(8,128)}, f32[512,512]{1,0:T(8,128)S(1)}, f32[512,384]{1,0:T(8,128)S(1)}, s32[]{:T(128)}) while((s32[]{:T(128)}, f32[512,384]{1,0:T(8,128)}, f32[512,512]{1,0:T(8,128)S(1)}, f32[512,384]{1,0:T(8,128)S(1)}, s32[]{:T(128)}) %tuple.78), condition=%wide.region_6.7_spmd, body=%wide.region_5.0_spmd.sunk | while | flops 1208156160 | bytes 8126565 | solution.py:92
  85.4 3.8 %fusion.37 = f32[512,384]{1,0:T(8,128)} fusion(f32[512,512]{1,0:T(8,128)S(1)} %get-tuple-element.295, f32[512,384]{1,0:T(8,128)} %get-tuple-element.289), kind=kOutput, calls=%fused_computation.57.clone.1 | convolution fusion | flops 1207959552 | bytes 2621440 | tf_op jit(solution)/shard_map/while/body/eval_jaxpr/dot_general | solution.py:17
  90.5 18.2 %collective-permute-done.1 = f32[512,384]{1,0:T(8,128)} collective-permute-done((f32[512,384]{1,0:T(8,128)}, f32[512,384]{1,0:T(8,128)}, u32[]{:S(2)}, u32[]{:S(2)}) %collective-permute-start.1) | collective-permute-done | bytes 786464 | tf_op jit(solution)/shard_map/while/body/eval_jaxpr/ppermute | solution.py:13
  108.7 2.1 sub.95
  110.8 3.8 %fusion.37 = f32[512,384]{1,0:T(8,128)} fusion(f32[512,512]{1,0:T(8,128)S(1)} %get-tuple-element.295, f32[512,384]{1,0:T(8,128)} %get-tuple-element.289), kind=kOutput, calls=%fused_computation.57.clone.1 | convolution fusion | flops 1207959552 | bytes 2621440 | tf_op jit(solution)/shard_map/while/body/eval_jaxpr/dot_general | solution.py:17
  116.0 16.8 %collective-permute-done.1 = f32[512,384]{1,0:T(8,128)} collective-permute-done((f32[512,384]{1,0:T(8,128)}, f32[512,384]{1,0:T(8,128)}, u32[]{:S(2)}, u32[]{:S(2)}) %collective-permute-start.1) | collective-permute-done | bytes 786464 | tf_op jit(solution)/shard_map/while/body/eval_jaxpr/ppermute | solution.py:13
  132.8 2.1 sub.95
  134.9 3.8 %fusion.37 = f32[512,384]{1,0:T(8,128)} fusion(f32[512,512]{1,0:T(8,128)S(1)} %get-tuple-element.295, f32[512,384]{1,0:T(8,128)} %get-tuple-element.289), kind=kOutput, calls=%fused_computation.57.clone.1 | convolution fusion | flops 1207959552 | bytes 2621440 | tf_op jit(solution)/shard_map/while/body/eval_jaxpr/dot_general | solution.py:17
  140.0 15.9 %collective-permute-done.1 = f32[512,384]{1,0:T(8,128)} collective-permute-done((f32[512,384]{1,0:T(8,128)}, f32[512,384]{1,0:T(8,128)}, u32[]{:S(2)}, u32[]{:S(2)}) %collective-permute-start.1) | collective-permute-done | bytes 786464 | tf_op jit(solution)/shard_map/while/body/eval_jaxpr/ppermute | solution.py:13
  155.9 2.1 sub.95
  158.0 1.4 copy.36
  159.4 4.5 %convolution_bitcast_fusion.1 = f32[2,3,128]{1,0,2:T(2,128)S(1)} fusion(f32[512,3,128]{0,2,1:T(8,128)S(1)} %bitcast.81, f32[512,2,128]{0,2,1:T(8,128)S(1)} %convert_subtract_fusion), kind=kOutput, calls=%fused_computation.9 | convolution fusion | flops 4718592 | bytes 1313792 | tf_op jit(solution)/shard_map/bit,bct->ict/dot_general | solution.py:94
  163.9 19.6 %psum.7 = f32[2,3,128]{1,0,2:T(2,128)S(1)} all-reduce(f32[2,3,128]{1,0,2:T(2,128)S(1)} %convolution_bitcast_fusion.1), channel_id=1, replica_groups=mesh['groups'=2,'front'=4,'batch'=2,'line'=2] {'front'}, use_global_device_ids=true, to_apply=%region_7.8 | all-reduce | flops 768 | bytes 6144 | tf_op jit(solution)/shard_map/psum | solution.py:97
  183.5 2.2 slice_reduce_fusion.2
  186.2 1.3 collective-permute-start.2
  189.1 5.4 %collective-permute-done.2 = f32[512,128]{1,0:T(8,128)S(1)} collective-permute-done((f32[512,128]{1,0:T(8,128)S(1)}, f32[512,128]{1,0:T(8,128)S(1)}, u32[]{:S(2)}, u32[]{:S(2)}) %collective-permute-start.2) | collective-permute-done | bytes 262176 | tf_op jit(solution)/shard_map/ppermute | solution.py:13
  196.7 1.9 fusion
  198.6 3.5 %all-to-all-start = ((f32[8,128,128]{2,1,0:T(8,128)}), f32[8,128,128]{2,1,0:T(8,128)S(1)}, u32[]{:S(2)}, u32[]{:S(2)}) async-start(f32[8,128,128]{2,1,0:T(8,128)} %bitcast.13), calls=%async_computation | async-start | bytes 1048576 | tf_op jit(solution)/shard_map/all_to_all | solution.py:116
  202.1 15.2 %all-to-all-done = f32[8,128,128]{2,1,0:T(8,128)S(1)} async-done(((f32[8,128,128]{2,1,0:T(8,128)}), f32[8,128,128]{2,1,0:T(8,128)S(1)}, u32[]{:S(2)}, u32[]{:S(2)}) %all-to-all-start) | async-done | bytes 524320 | tf_op jit(solution)/shard_map/all_to_all | solution.py:116
  217.4 25.2 %while.34 = (s32[]{:T(128)}, f32[128,128]{1,0:T(8,128)S(1)}, f32[32,32,128]{2,1,0:T(8,128)S(1)}, f32[128]{0:T(128)S(1)}, f32[128]{0:T(128)S(1)}, /*index=5*/f32[1,1,128]{2,1,0:T(1,128)S(1)}, s32[]{:T(128)}, s32[]{:T(128)}) while((s32[]{:T(128)}, f32[128,128]{1,0:T(8,128)S(1)}, f32[32,32,128]{2,1,0:T(8,128)S(1)}, ...), condition=%wide.region_10.11_spmd.clone, body=%wide.region_8.10_spmd.clone.sunk | while | flops 2113539 | bytes 312931 | solution.py:125
  (152 shorter events, 37.3 us)
Async XLA Ops:
  0.6 77.8 %copy-start = (f32[512,512]{1,0:T(8,128)S(1)}, f32[512,512]{1,0:T(8,128)}, u32[]{:S(2)}) copy-start(f32[512,512]{1,0:T(8,128)} %param.24) | copy-start | bytes 3145732
  3.0 1.5 copy-start.1
  4.5 22.0 %collective-permute-start = (f32[512,384]{1,0:T(8,128)}, f32[512,384]{1,0:T(8,128)}, u32[]{:S(2)}, u32[]{:S(2)}) collective-permute-start(f32[512,384]{1,0:T(8,128)} %get-tuple-element.274), channel_id=1, source_target_pairs={{0,4},{4,8},{8,12},{1,5},{5,9},{9,13},{2,6},{6,10},{10,14},{3,7},{... | collective-permute-start | bytes 2359304 | tf_op jit(solution)/shard_map/while/body/eval_jaxpr/ppermute | solution.py:13
  30.4 20.6 %collective-permute-start = (f32[512,384]{1,0:T(8,128)}, f32[512,384]{1,0:T(8,128)}, u32[]{:S(2)}, u32[]{:S(2)}) collective-permute-start(f32[512,384]{1,0:T(8,128)} %get-tuple-element.274), channel_id=1, source_target_pairs={{0,4},{4,8},{8,12},{1,5},{5,9},{9,13},{2,6},{6,10},{10,14},{3,7},{... | collective-permute-start | bytes 2359304 | tf_op jit(solution)/shard_map/while/body/eval_jaxpr/ppermute | solution.py:13
  54.9 19.7 %collective-permute-start = (f32[512,384]{1,0:T(8,128)}, f32[512,384]{1,0:T(8,128)}, u32[]{:S(2)}, u32[]{:S(2)}) collective-permute-start(f32[512,384]{1,0:T(8,128)} %get-tuple-element.274), channel_id=1, source_target_pairs={{0,4},{4,8},{8,12},{1,5},{5,9},{9,13},{2,6},{6,10},{10,14},{3,7},{... | collective-permute-start | bytes 2359304 | tf_op jit(solution)/shard_map/while/body/eval_jaxpr/ppermute | solution.py:13
  89.2 19.5 %collective-permute-start.1 = (f32[512,384]{1,0:T(8,128)}, f32[512,384]{1,0:T(8,128)}, u32[]{:S(2)}, u32[]{:S(2)}) collective-permute-start(f32[512,384]{1,0:T(8,128)} %fusion.37), channel_id=1, source_target_pairs={{4,0},{8,4},{12,8},{5,1},{9,5},{13,9},{6,2},{10,6},{14,10},{7,3},{... | collective-permute-start | bytes 2359304 | tf_op jit(solution)/shard_map/while/body/eval_jaxpr/ppermute | solution.py:13
  114.7 18.1 %collective-permute-start.1 = (f32[512,384]{1,0:T(8,128)}, f32[512,384]{1,0:T(8,128)}, u32[]{:S(2)}, u32[]{:S(2)}) collective-permute-start(f32[512,384]{1,0:T(8,128)} %fusion.37), channel_id=1, source_target_pairs={{4,0},{8,4},{12,8},{5,1},{9,5},{13,9},{6,2},{10,6},{14,10},{7,3},{... | collective-permute-start | bytes 2359304 | tf_op jit(solution)/shard_map/while/body/eval_jaxpr/ppermute | solution.py:13
  138.7 17.2 %collective-permute-start.1 = (f32[512,384]{1,0:T(8,128)}, f32[512,384]{1,0:T(8,128)}, u32[]{:S(2)}, u32[]{:S(2)}) collective-permute-start(f32[512,384]{1,0:T(8,128)} %fusion.37), channel_id=1, source_target_pairs={{4,0},{8,4},{12,8},{5,1},{9,5},{13,9},{6,2},{10,6},{14,10},{7,3},{... | collective-permute-start | bytes 2359304 | tf_op jit(solution)/shard_map/while/body/eval_jaxpr/ppermute | solution.py:13
  163.9 21.8 %copy-start.8 = (f32[2,128]{1,0:T(2,128)S(1)}, f32[2,128]{1,0:T(2,128)}, u32[]{:S(2)}) copy-start(f32[2,128]{1,0:T(2,128)} %param.22) | copy-start | bytes 3076
  185.9 1.7 copy-start.6
  185.9 1.7 copy-start.7
  185.9 1.7 copy-start.4
  186.2 9.4 %copy-start.2 = (f32[512,128]{1,0:T(8,128)}, f32[512,128]{1,0:T(8,128)S(1)}, u32[]{:S(2)}) copy-start(f32[512,128]{1,0:T(8,128)S(1)} %bitcast_subtract_fusion) | copy-start | bytes 786436
  186.2 8.3 %collective-permute-start.2 = (f32[512,128]{1,0:T(8,128)S(1)}, f32[512,128]{1,0:T(8,128)S(1)}, u32[]{:S(2)}, u32[]{:S(2)}) collective-permute-start(f32[512,128]{1,0:T(8,128)S(1)} %bitcast_subtract_fusion), channel_id=1, source_target_pairs={{4,0},{8,4},{12,8},{5,1},{9,5},{13,9},{6,2},{10,6},{14,10},{7,3},{... | collective-permute-start | bytes 786440 | tf_op jit(solution)/shard_map/ppermute | solution.py:13
  195.6 1.1 copy-start.5
  196.7 5.5 %copy-start.10 = (f32[128]{0:T(128)S(1)}, f32[128]{0:T(128)}, u32[]{:S(2)}) copy-start(f32[128]{0:T(128)} %param.30) | copy-start | bytes 1540
  196.7 20.7 %copy-start.9 = (f32[128]{0:T(128)S(1)}, f32[128]{0:T(128)}, u32[]{:S(2)}) copy-start(f32[128]{0:T(128)} %param.29) | copy-start | bytes 1540
  198.6 18.8 %all-to-all-start = ((f32[8,128,128]{2,1,0:T(8,128)}), f32[8,128,128]{2,1,0:T(8,128)S(1)}, u32[]{:S(2)}, u32[]{:S(2)}) async-start(f32[8,128,128]{2,1,0:T(8,128)} %bitcast.13), calls=%async_computation | async-start | bytes 1048576 | tf_op jit(solution)/shard_map/all_to_all | solution.py:116
  217.4 25.2 %copy-start.3 = (bf16[128,128]{1,0:T(8,128)(2,1)S(1)}, bf16[128,128]{1,0:T(8,128)(2,1)}, u32[]{:S(2)}) copy-start(bf16[128,128]{1,0:T(8,128)(2,1)} %param.31) | copy-start | bytes 98308
where the time goes:
time: 244 us; the launch traced here: 243 us
  waiting for transfers between devices  118 us (48%)
  matrix products  34.9 us (14%)
  other arithmetic  32.3 us (13%)
  starting transfers between devices  24.9 us (10%)
  blocking collectives  19.6 us (8%)
  local copies, waits for them, and re-layouts  11.7 us (5%)
    ppermute x7, waiting for transfers between devices, from_behind(): return lax.ppermute(value, axis, pairs)  102 us
    dot_general x8, matrix products, product(): jnp.dot(operand, against, precision=lax.Precision.HIGHEST, preferred_elem...  29.7 us
    reduce_sum x32, other arithmetic, accumulate(): jnp.sum(centered_tanh(slot_block, in_weight, in_bias), axis=0)  23 us
    ppermute x7, starting transfers between devices, from_behind(): return lax.ppermute(value, axis, pairs)  21.5 us
    psum x1, blocking collectives, body(): terms = lax.psum(local_terms, 'front')  19.6 us
    all_to_all x1, waiting for transfers between devices, body(): lax.all_to_all(outgoing, ('front', 'line'), split_axis=0, concat_axis=0,...  15.2 us
    sub x3, other arithmetic, upper_step(): return pivoted - arrived  6.31 us
  transfers between devices with their start and end apart: 8, of which 8 were waited for; matrix products, arithmetic and copies ran while one was open for 1% of the time, Pallas kernels for 0%

commit v1 on v0

--- a/solution.py
+++ b/solution.py
@@ -5,6 +5,14 @@
 
 K = 2
 BR_DEV = 512
+
+
+def added_up(block, mesh_axis):
+    size, total = (lax.axis_size(mesh_axis), block)
+    for far in [1 << k for k in range(size.bit_length() - 1)]:
+        swap = [(i, i ^ far) for i in range(size)]
+        total = total + lax.ppermute(total, mesh_axis, swap)
+    return total
 
 
 def from_behind(value, axis, by):
@@ -94,7 +102,7 @@
     local_terms = jnp.einsum(
         "bit,bct->ict", incidence, solved_cols, precision=lax.Precision.HIGHEST
     )
-    terms = lax.psum(local_terms, "front")
+    terms = added_up(local_terms, "front")
     weights = capacitance_solve(terms, switch_susc)
     angles = solved_cols[:, 0, :] - jnp.einsum(
         "bit,it->bt", solved_cols[:, 1:, :], weights, precision=lax.Precision.HIGHEST

time: 244 us -> 239 us (0.980)
  blocking collectives: 19.6 us -> 0 us
  waiting for transfers between devices: 118 us -> 129 us
  starting transfers between devices: 24.9 us -> 27.5 us
    psum x1 -> x0, blocking collectives: 19.6 us -> none  [body(): terms = lax.psum(local_terms, 'front')]
    ppermute x0 -> x2, waiting for transfers between devices: none -> 9.98 us  [added_up(): total = total + lax.ppermute(total, mesh_axis, swap)]
    ppermute x0 -> x2, starting transfers between devices: none -> 2.53 us  [added_up(): total = total + lax.ppermute(total, mesh_axis, swap)]
  transfers between devices with their start and end apart: 8 -> 10, of which waited for: 8 -> 10; matrix products, arithmetic and copies ran while one was open for 1% -> 1% of each run, Pallas kernels for 0% -> 0%
where the time goes in v1:
time: 239 us; the launch traced here: 238 us
  waiting for transfers between devices  129 us (54%)
  matrix products  34.9 us (15%)
  other arithmetic  32.6 us (14%)
  starting transfers between devices  27.5 us (12%)
  local copies, waits for them, and re-layouts  11.6 us (5%)
    ppermute x7, waiting for transfers between devices, from_behind(): return lax.ppermute(value, axis, pairs)  104 us
    dot_general x8, matrix products, product(): jnp.dot(operand, against, precision=lax.Precision.HIGHEST, preferred_elem...  29.7 us
    reduce_sum x32, other arithmetic, accumulate(): jnp.sum(centered_tanh(slot_block, in_weight, in_bias), axis=0)  23 us
    ppermute x7, starting transfers between devices, from_behind(): return lax.ppermute(value, axis, pairs)  21.5 us
    all_to_all x1, waiting for transfers between devices, body(): lax.all_to_all(outgoing, ('front', 'line'), split_axis=0, concat_axis=0,...  15.2 us
    ppermute x2, waiting for transfers between devices, added_up(): total = total + lax.ppermute(total, mesh_axis, swap)  9.98 us
    sub x3, other arithmetic, upper_step(): return pivoted - arrived  6.31 us
  transfers between devices with their start and end apart: 10, of which 10 were waited for; matrix products, arithmetic and copies ran while one was open for 1% of the time, Pallas kernels for 0%

profile of v1, /device:TPU:0, one launch (start us, length us, event | category | flops | bytes accessed | tf_op | source)
XLA Modules:
  0.0 238.1 jit_solution(14995552855686193580)
XLA Ops:
  4.5 73.9 %while.32 = (s32[]{:T(128)}, f32[512,384]{1,0:T(8,128)}, f32[512,512]{1,0:T(8,128)S(1)}, f32[512,384]{1,0:T(8,128)S(1)}, s32[]{:T(128)}) while((s32[]{:T(128)}, f32[512,384]{1,0:T(8,128)}, f32[512,512]{1,0:T(8,128)S(1)}, f32[512,384]{1,0:T(8,128)S(1)}, s32[]{:T(128)}) %tuple.77), condition=%wide.region_4.0_spmd, body=%wide.region_3.0_spmd.sunk | while | flops 1208156160 | bytes 6553701 | solution.py:93
  4.5 5.8 %collective-permute-start = (f32[512,384]{1,0:T(8,128)}, f32[512,384]{1,0:T(8,128)}, u32[]{:S(2)}, u32[]{:S(2)}) collective-permute-start(f32[512,384]{1,0:T(8,128)} %get-tuple-element.274), channel_id=1, source_target_pairs={{0,4},{4,8},{8,12},{1,5},{5,9},{9,13},{2,6},{6,10},{10,14},{3,7},{... | collective-permute-start | bytes 2359304 | tf_op jit(solution)/shard_map/while/body/eval_jaxpr/ppermute | solution.py:21
  10.3 16.2 %collective-permute-done = f32[512,384]{1,0:T(8,128)} collective-permute-done((f32[512,384]{1,0:T(8,128)}, f32[512,384]{1,0:T(8,128)}, u32[]{:S(2)}, u32[]{:S(2)}) %collective-permute-start) | collective-permute-done | bytes 786464 | tf_op jit(solution)/shard_map/while/body/eval_jaxpr/ppermute | solution.py:21
  26.6 3.8 %convolution_subtract_fusion.2 = f32[512,384]{1,0:T(8,128)} fusion(f32[512,384]{1,0:T(8,128)S(1)} %get-tuple-element.281, f32[512,512]{1,0:T(8,128)S(1)} %get-tuple-element.280, f32[512,384]{1,0:T(8,128)} %collective-permute-done), kind=kOutput, calls=%fused_computation.2.clone.1 | convolution fusion | flops 1208156160 | bytes 3407872 | tf_op jit(solution)/shard_map/while/body/eval_jaxpr/dot_general | solution.py:25
  30.4 5.3 %collective-permute-start = (f32[512,384]{1,0:T(8,128)}, f32[512,384]{1,0:T(8,128)}, u32[]{:S(2)}, u32[]{:S(2)}) collective-permute-start(f32[512,384]{1,0:T(8,128)} %get-tuple-element.274), channel_id=1, source_target_pairs={{0,4},{4,8},{8,12},{1,5},{5,9},{9,13},{2,6},{6,10},{10,14},{3,7},{... | collective-permute-start | bytes 2359304 | tf_op jit(solution)/shard_map/while/body/eval_jaxpr/ppermute | solution.py:21
  35.7 15.4 %collective-permute-done = f32[512,384]{1,0:T(8,128)} collective-permute-done((f32[512,384]{1,0:T(8,128)}, f32[512,384]{1,0:T(8,128)}, u32[]{:S(2)}, u32[]{:S(2)}) %collective-permute-start) | collective-permute-done | bytes 786464 | tf_op jit(solution)/shard_map/while/body/eval_jaxpr/ppermute | solution.py:21
  51.0 3.8 %convolution_subtract_fusion.2 = f32[512,384]{1,0:T(8,128)} fusion(f32[512,384]{1,0:T(8,128)S(1)} %get-tuple-element.281, f32[512,512]{1,0:T(8,128)S(1)} %get-tuple-element.280, f32[512,384]{1,0:T(8,128)} %collective-permute-done), kind=kOutput, calls=%fused_computation.2.clone.1 | convolution fusion | flops 1208156160 | bytes 3407872 | tf_op jit(solution)/shard_map/while/body/eval_jaxpr/dot_general | solution.py:25
  54.9 5.3 %collective-permute-start = (f32[512,384]{1,0:T(8,128)}, f32[512,384]{1,0:T(8,128)}, u32[]{:S(2)}, u32[]{:S(2)}) collective-permute-start(f32[512,384]{1,0:T(8,128)} %get-tuple-element.274), channel_id=1, source_target_pairs={{0,4},{4,8},{8,12},{1,5},{5,9},{9,13},{2,6},{6,10},{10,14},{3,7},{... | collective-permute-start | bytes 2359304 | tf_op jit(solution)/shard_map/while/body/eval_jaxpr/ppermute | solution.py:21
  60.1 14.4 %collective-permute-done = f32[512,384]{1,0:T(8,128)} collective-permute-done((f32[512,384]{1,0:T(8,128)}, f32[512,384]{1,0:T(8,128)}, u32[]{:S(2)}, u32[]{:S(2)}) %collective-permute-start) | collective-permute-done | bytes 786464 | tf_op jit(solution)/shard_map/while/body/eval_jaxpr/ppermute | solution.py:21
  74.5 3.8 %convolution_subtract_fusion.2 = f32[512,384]{1,0:T(8,128)} fusion(f32[512,384]{1,0:T(8,128)S(1)} %get-tuple-element.281, f32[512,512]{1,0:T(8,128)S(1)} %get-tuple-element.280, f32[512,384]{1,0:T(8,128)} %collective-permute-done), kind=kOutput, calls=%fused_computation.2.clone.1 | convolution fusion | flops 1208156160 | bytes 3407872 | tf_op jit(solution)/shard_map/while/body/eval_jaxpr/dot_general | solution.py:25
  78.4 4.7 %convolution_bitcast_fusion = f32[512,384]{0,1:T(8,128)} fusion(f32[512,384]{1,0:T(8,128)} %get-tuple-element.98, f32[512,512]{1,0:T(8,128)S(1)} %copy-done), kind=kOutput, calls=%fused_computation.8 | convolution fusion | flops 1207959552 | bytes 2621440 | tf_op jit(solution)/shard_map/dot_general | solution.py:25
  83.1 1.4 copy.34
  85.4 72.7 %while.33 = (s32[]{:T(128)}, f32[512,384]{1,0:T(8,128)}, f32[512,512]{1,0:T(8,128)S(1)}, f32[512,384]{1,0:T(8,128)S(1)}, s32[]{:T(128)}) while((s32[]{:T(128)}, f32[512,384]{1,0:T(8,128)}, f32[512,512]{1,0:T(8,128)S(1)}, f32[512,384]{1,0:T(8,128)S(1)}, s32[]{:T(128)}) %tuple.78), condition=%wide.region_6.7_spmd, body=%wide.region_5.6_spmd.sunk | while | flops 1208156160 | bytes 8126565 | solution.py:100
  85.4 3.8 %fusion.37 = f32[512,384]{1,0:T(8,128)} fusion(f32[512,512]{1,0:T(8,128)S(1)} %get-tuple-element.295, f32[512,384]{1,0:T(8,128)} %get-tuple-element.289), kind=kOutput, calls=%fused_computation.57.clone.1 | convolution fusion | flops 1207959552 | bytes 2621440 | tf_op jit(solution)/shard_map/while/body/eval_jaxpr/dot_general | solution.py:25
  90.5 18.2 %collective-permute-done.1 = f32[512,384]{1,0:T(8,128)} collective-permute-done((f32[512,384]{1,0:T(8,128)}, f32[512,384]{1,0:T(8,128)}, u32[]{:S(2)}, u32[]{:S(2)}) %collective-permute-start.1) | collective-permute-done | bytes 786464 | tf_op jit(solution)/shard_map/while/body/eval_jaxpr/ppermute | solution.py:21
  108.7 2.1 sub.95
  110.8 3.8 %fusion.37 = f32[512,384]{1,0:T(8,128)} fusion(f32[512,512]{1,0:T(8,128)S(1)} %get-tuple-element.295, f32[512,384]{1,0:T(8,128)} %get-tuple-element.289), kind=kOutput, calls=%fused_computation.57.clone.1 | convolution fusion | flops 1207959552 | bytes 2621440 | tf_op jit(solution)/shard_map/while/body/eval_jaxpr/dot_general | solution.py:25
  116.0 16.8 %collective-permute-done.1 = f32[512,384]{1,0:T(8,128)} collective-permute-done((f32[512,384]{1,0:T(8,128)}, f32[512,384]{1,0:T(8,128)}, u32[]{:S(2)}, u32[]{:S(2)}) %collective-permute-start.1) | collective-permute-done | bytes 786464 | tf_op jit(solution)/shard_map/while/body/eval_jaxpr/ppermute | solution.py:21
  132.8 2.1 sub.95
  134.9 3.8 %fusion.37 = f32[512,384]{1,0:T(8,128)} fusion(f32[512,512]{1,0:T(8,128)S(1)} %get-tuple-element.295, f32[512,384]{1,0:T(8,128)} %get-tuple-element.289), kind=kOutput, calls=%fused_computation.57.clone.1 | convolution fusion | flops 1207959552 | bytes 2621440 | tf_op jit(solution)/shard_map/while/body/eval_jaxpr/dot_general | solution.py:25
  140.0 15.9 %collective-permute-done.1 = f32[512,384]{1,0:T(8,128)} collective-permute-done((f32[512,384]{1,0:T(8,128)}, f32[512,384]{1,0:T(8,128)}, u32[]{:S(2)}, u32[]{:S(2)}) %collective-permute-start.1) | collective-permute-done | bytes 786464 | tf_op jit(solution)/shard_map/while/body/eval_jaxpr/ppermute | solution.py:21
  155.9 2.1 sub.95
  158.0 1.4 copy.36
  159.5 4.5 %convolution_bitcast_fusion.1 = f32[2,3,128]{1,0,2:T(2,128)S(1)} fusion(f32[512,3,128]{0,2,1:T(8,128)S(1)} %bitcast.81, f32[512,2,128]{0,2,1:T(8,128)S(1)} %convert_subtract_fusion), kind=kOutput, calls=%fused_computation.9 | convolution fusion | flops 4718592 | bytes 1313792 | tf_op jit(solution)/shard_map/bit,bct->ict/dot_general | solution.py:102
  166.9 3.1 %collective-permute-done.2 = f32[2,3,128]{1,0,2:T(2,128)S(1)} collective-permute-done((f32[2,3,128]{1,0,2:T(2,128)S(1)}, f32[2,3,128]{1,0,2:T(2,128)S(1)}, u32[]{:S(2)}, u32[]{:S(2)}) %collective-permute-start.2) | collective-permute-done | bytes 3104 | tf_op jit(solution)/shard_map/ppermute | solution.py:14
  171.5 6.9 %collective-permute-done.3 = f32[2,3,128]{1,0,2:T(2,128)S(1)} collective-permute-done((f32[2,3,128]{1,0,2:T(2,128)S(1)}, f32[2,3,128]{1,0,2:T(2,128)S(1)}, u32[]{:S(2)}, u32[]{:S(2)}) %collective-permute-start.3) | collective-permute-done | bytes 3104 | tf_op jit(solution)/shard_map/ppermute | solution.py:14
  178.5 2.2 slice_reduce_fusion.2
  182.3 6.9 %collective-permute-done.4 = f32[512,128]{1,0:T(8,128)S(1)} collective-permute-done((f32[512,128]{1,0:T(8,128)S(1)}, f32[512,128]{1,0:T(8,128)S(1)}, u32[]{:S(2)}, u32[]{:S(2)}) %collective-permute-start.4) | collective-permute-done | bytes 262176 | tf_op jit(solution)/shard_map/ppermute | solution.py:21
  191.5 1.9 fusion
  193.4 3.5 %all-to-all-start = ((f32[8,128,128]{2,1,0:T(8,128)}), f32[8,128,128]{2,1,0:T(8,128)S(1)}, u32[]{:S(2)}, u32[]{:S(2)}) async-start(f32[8,128,128]{2,1,0:T(8,128)} %bitcast.13), calls=%async_computation | async-start | bytes 1048576 | tf_op jit(solution)/shard_map/all_to_all | solution.py:124
  196.9 15.2 %all-to-all-done = f32[8,128,128]{2,1,0:T(8,128)S(1)} async-done(((f32[8,128,128]{2,1,0:T(8,128)}), f32[8,128,128]{2,1,0:T(8,128)S(1)}, u32[]{:S(2)}, u32[]{:S(2)}) %all-to-all-start) | async-done | bytes 524320 | tf_op jit(solution)/shard_map/all_to_all | solution.py:124
  212.2 25.2 %while.34 = (s32[]{:T(128)}, f32[128,128]{1,0:T(8,128)S(1)}, f32[32,32,128]{2,1,0:T(8,128)S(1)}, f32[128]{0:T(128)S(1)}, f32[128]{0:T(128)S(1)}, /*index=5*/f32[1,1,128]{2,1,0:T(1,128)S(1)}, s32[]{:T(128)}, s32[]{:T(128)}) while((s32[]{:T(128)}, f32[128,128]{1,0:T(8,128)S(1)}, f32[32,32,128]{2,1,0:T(8,128)S(1)}, ...), condition=%wide.region_9.10_spmd.clone, body=%wide.region_7.9_spmd.clone.sunk | while | flops 2113539 | bytes 312931 | solution.py:133
  (157 shorter events, 41.4 us)
Async XLA Ops:
  0.6 77.8 %copy-start = (f32[512,512]{1,0:T(8,128)S(1)}, f32[512,512]{1,0:T(8,128)}, u32[]{:S(2)}) copy-start(f32[512,512]{1,0:T(8,128)} %param.24) | copy-start | bytes 3145732
  3.0 1.5 copy-start.1
  4.5 22.0 %collective-permute-start = (f32[512,384]{1,0:T(8,128)}, f32[512,384]{1,0:T(8,128)}, u32[]{:S(2)}, u32[]{:S(2)}) collective-permute-start(f32[512,384]{1,0:T(8,128)} %get-tuple-element.274), channel_id=1, source_target_pairs={{0,4},{4,8},{8,12},{1,5},{5,9},{9,13},{2,6},{6,10},{10,14},{3,7},{... | collective-permute-start | bytes 2359304 | tf_op jit(solution)/shard_map/while/body/eval_jaxpr/ppermute | solution.py:21
  30.4 20.6 %collective-permute-start = (f32[512,384]{1,0:T(8,128)}, f32[512,384]{1,0:T(8,128)}, u32[]{:S(2)}, u32[]{:S(2)}) collective-permute-start(f32[512,384]{1,0:T(8,128)} %get-tuple-element.274), channel_id=1, source_target_pairs={{0,4},{4,8},{8,12},{1,5},{5,9},{9,13},{2,6},{6,10},{10,14},{3,7},{... | collective-permute-start | bytes 2359304 | tf_op jit(solution)/shard_map/while/body/eval_jaxpr/ppermute | solution.py:21
  54.9 19.7 %collective-permute-start = (f32[512,384]{1,0:T(8,128)}, f32[512,384]{1,0:T(8,128)}, u32[]{:S(2)}, u32[]{:S(2)}) collective-permute-start(f32[512,384]{1,0:T(8,128)} %get-tuple-element.274), channel_id=1, source_target_pairs={{0,4},{4,8},{8,12},{1,5},{5,9},{9,13},{2,6},{6,10},{10,14},{3,7},{... | collective-permute-start | bytes 2359304 | tf_op jit(solution)/shard_map/while/body/eval_jaxpr/ppermute | solution.py:21
  89.2 19.5 %collective-permute-start.1 = (f32[512,384]{1,0:T(8,128)}, f32[512,384]{1,0:T(8,128)}, u32[]{:S(2)}, u32[]{:S(2)}) collective-permute-start(f32[512,384]{1,0:T(8,128)} %fusion.37), channel_id=1, source_target_pairs={{4,0},{8,4},{12,8},{5,1},{9,5},{13,9},{6,2},{10,6},{14,10},{7,3},{... | collective-permute-start | bytes 2359304 | tf_op jit(solution)/shard_map/while/body/eval_jaxpr/ppermute | solution.py:21
  114.7 18.1 %collective-permute-start.1 = (f32[512,384]{1,0:T(8,128)}, f32[512,384]{1,0:T(8,128)}, u32[]{:S(2)}, u32[]{:S(2)}) collective-permute-start(f32[512,384]{1,0:T(8,128)} %fusion.37), channel_id=1, source_target_pairs={{4,0},{8,4},{12,8},{5,1},{9,5},{13,9},{6,2},{10,6},{14,10},{7,3},{... | collective-permute-start | bytes 2359304 | tf_op jit(solution)/shard_map/while/body/eval_jaxpr/ppermute | solution.py:21
  138.7 17.2 %collective-permute-start.1 = (f32[512,384]{1,0:T(8,128)}, f32[512,384]{1,0:T(8,128)}, u32[]{:S(2)}, u32[]{:S(2)}) collective-permute-start(f32[512,384]{1,0:T(8,128)} %fusion.37), channel_id=1, source_target_pairs={{4,0},{8,4},{12,8},{5,1},{9,5},{13,9},{6,2},{10,6},{14,10},{7,3},{... | collective-permute-start | bytes 2359304 | tf_op jit(solution)/shard_map/while/body/eval_jaxpr/ppermute | solution.py:21
  159.4 5.8 %copy-start.4 = (s32[512,1]{0,1:T(1,128)S(1)}, s32[512,1]{0,1:T(1,128)}, u32[]{:S(2)}) copy-start(s32[512,1]{0,1:T(1,128)} %param.28) | copy-start | bytes 6148
  159.4 7.3 %copy-start.6 = (s32[512]{0:T(512)S(1)}, s32[512]{0:T(512)}, u32[]{:S(2)}) copy-start(s32[512]{0:T(512)} %param.26) | copy-start | bytes 6148
  159.5 7.3 %copy-start.7 = (s32[512]{0:T(512)S(1)}, s32[512]{0:T(512)}, u32[]{:S(2)}) copy-start(s32[512]{0:T(512)} %param.25) | copy-start | bytes 6148
  164.0 6.0 %collective-permute-start.2 = (f32[2,3,128]{1,0,2:T(2,128)S(1)}, f32[2,3,128]{1,0,2:T(2,128)S(1)}, u32[]{:S(2)}, u32[]{:S(2)}) collective-permute-start(f32[2,3,128]{1,0,2:T(2,128)S(1)} %convolution_bitcast_fusion.1), channel_id=1, source_target_pairs={{0,4},{4,0},{8,12},{12,8},{1,5},{5,1},{9,13},{13,9},{2,6},{6,2},{1... | collective-permute-start | bytes 9224 | tf_op jit(solution)/shard_map/ppermute | solution.py:14
  166.9 13.8 %copy-start.8 = (f32[2,128]{1,0:T(2,128)S(1)}, f32[2,128]{1,0:T(2,128)}, u32[]{:S(2)}) copy-start(f32[2,128]{1,0:T(2,128)} %param.22) | copy-start | bytes 3076
  170.0 8.4 %collective-permute-start.3 = (f32[2,3,128]{1,0,2:T(2,128)S(1)}, f32[2,3,128]{1,0,2:T(2,128)S(1)}, u32[]{:S(2)}, u32[]{:S(2)}) collective-permute-start(f32[2,3,128]{1,0,2:T(2,128)S(1)} %add.66), channel_id=1, source_target_pairs={{0,8},{4,12},{8,0},{12,4},{1,9},{5,13},{9,1},{13,5},{2,10},{6,14},... | collective-permute-start | bytes 9224 | tf_op jit(solution)/shard_map/ppermute | solution.py:14
  181.0 9.4 %copy-start.2 = (f32[512,128]{1,0:T(8,128)}, f32[512,128]{1,0:T(8,128)S(1)}, u32[]{:S(2)}) copy-start(f32[512,128]{1,0:T(8,128)S(1)} %bitcast_subtract_fusion) | copy-start | bytes 786436
  181.0 8.3 %collective-permute-start.4 = (f32[512,128]{1,0:T(8,128)S(1)}, f32[512,128]{1,0:T(8,128)S(1)}, u32[]{:S(2)}, u32[]{:S(2)}) collective-permute-start(f32[512,128]{1,0:T(8,128)S(1)} %bitcast_subtract_fusion), channel_id=1, source_target_pairs={{4,0},{8,4},{12,8},{5,1},{9,5},{13,9},{6,2},{10,6},{14,10},{7,3},{... | collective-permute-start | bytes 786440 | tf_op jit(solution)/shard_map/ppermute | solution.py:21
  190.4 1.1 copy-start.5
  191.4 5.5 %copy-start.10 = (f32[128]{0:T(128)S(1)}, f32[128]{0:T(128)}, u32[]{:S(2)}) copy-start(f32[128]{0:T(128)} %param.30) | copy-start | bytes 1540
  191.4 20.7 %copy-start.9 = (f32[128]{0:T(128)S(1)}, f32[128]{0:T(128)}, u32[]{:S(2)}) copy-start(f32[128]{0:T(128)} %param.29) | copy-start | bytes 1540
  193.4 18.8 %all-to-all-start = ((f32[8,128,128]{2,1,0:T(8,128)}), f32[8,128,128]{2,1,0:T(8,128)S(1)}, u32[]{:S(2)}, u32[]{:S(2)}) async-start(f32[8,128,128]{2,1,0:T(8,128)} %bitcast.13), calls=%async_computation | async-start | bytes 1048576 | tf_op jit(solution)/shard_map/all_to_all | solution.py:124
  212.2 25.2 %copy-start.3 = (bf16[128,128]{1,0:T(8,128)(2,1)S(1)}, bf16[128,128]{1,0:T(8,128)(2,1)}, u32[]{:S(2)}) copy-start(bf16[128,128]{1,0:T(8,128)(2,1)} %param.31) | copy-start | bytes 98308
